TPU v7x, 256 devices: a whole 4x4x8 slice. The times are simulated.
256 devices in a mesh: gx: 32 (over x, z), gy: 8 (over y, core).
Axes of the slice: x: 4, y: 4, z: 8, core: 2. Of those that a mesh axis runs over, the one named last changes fastest.
Arguments:
- probes: bfloat16 [64, 256, 128, 128], P(None, 'gx', 'gy'), may hold values from -6 to 6
- permeability: float32 [256, 128, 128], P('gx', 'gy'), may hold values from 0.2 to 5
- absorption: float32 [256, 128, 128], P('gx', 'gy'), may hold values from 0.3 to 3
- sensitivity: float32 [256, 128, 128], P('gx', 'gy'), may hold values from -6 to 6
- observe_weight: float32 [256, 128, 128], P('gx', 'gy'), may hold values from 1 to 10
Outputs:
- q_basis: float32 [64, 256, 128, 128], P(None, 'gx', 'gy')
- r_factor: float32 [64, 64], replicated
All inputs are finite; a program needn't handle non-finite values.
Results may differ from a plain program's by a relative error of at most 0.0003.
Values sent between devices are 32-bit elements; how exact they have to be, the bound alone decides.
A program may use at most 128 MiB of HBM per device.

v0:
```python
import jax
import jax.numpy as jnp
from jax import lax
from jax.sharding import PartitionSpec as P

SWEEPS = 4


def padded_2(shard, sides, width):
    for axis, dim in sides:
        peers, length = (lax.axis_size(axis), shard.shape[dim])
        up = [(i, (i + 1) % peers) for i in range(peers - 1)]
        down = [(j, i) for i, j in up]
        last = lax.slice_in_dim(shard, length - width, length, axis=dim)
        first = lax.slice_in_dim(shard, 0, width, axis=dim)
        before = lax.ppermute(last, axis, up)
        after = lax.ppermute(first, axis, down)
        shard = jnp.concatenate([before, shard, after], axis=dim)
    return shard


def face_terms(kpad, absorption):
    center = kpad[1:-1, 1:-1]
    x_low = 0.5 * (center + kpad[:-2, 1:-1])
    x_high = 0.5 * (center + kpad[2:, 1:-1])
    y_low = 0.5 * (center + kpad[1:-1, :-2])
    y_high = 0.5 * (center + kpad[1:-1, 2:])
    zpad = jnp.pad(center, ((0, 0), (0, 0), (1, 1)))
    z_low = 0.5 * (center + zpad[:, :, :-2])
    z_high = 0.5 * (center + zpad[:, :, 2:])
    diag = absorption + x_low + x_high + y_low + y_high + z_low + z_high
    return ((x_low, x_high, y_low, y_high, z_low, z_high), diag)


def sweep(field, padded, rhs, coefs, diag):
    x_low, x_high, y_low, y_high, z_low, z_high = coefs
    zpad = jnp.pad(field, ((0, 0), (0, 0), (0, 0), (1, 1)))
    total = x_low * padded[:, :-2, 1:-1] + x_high * padded[:, 2:, 1:-1]
    total = total + y_low * padded[:, 1:-1, :-2] + y_high * padded[:, 1:-1, 2:]
    total = total + z_low * zpad[..., :-2] + z_high * zpad[..., 2:]
    return 0.2 * field + 0.8 * (rhs + total) / diag


def single_solve(rhs, coefs, diag):
    field = 0.8 * rhs / diag
    for step in range(SWEEPS - 1):
        padded = padded_2(field, (("gx", 1), ("gy", 2)), 1)
        field = sweep(field, padded, rhs, coefs, diag)
    return field


def lower_inverse(lower):
    width = lower.shape[0]
    identity = jnp.eye(width, dtype=jnp.float32)

    def row_step(index, inverse):
        row = lax.dynamic_slice_in_dim(lower, index, 1, 0)
        pivot = lax.dynamic_slice(lower, (index, index), (1, 1))
        unit = lax.dynamic_slice_in_dim(identity, index, 1, 0)
        partial_sum = jnp.dot(
            row, inverse, precision=lax.Precision.HIGHEST, preferred_element_type=jnp.float32
        )
        new_row = (unit - partial_sum) / pivot
        return lax.dynamic_update_slice_in_dim(inverse, new_row, index, 0)

    return lax.fori_loop(0, width, row_step, jnp.zeros((width, width), jnp.float32))


def body(probes, permeability, absorption, sensitivity, observe_weight):
    count, width_x, width_y, width_z = probes.shape
    total_cells = width_x * lax.axis_size("gx") * width_y * lax.axis_size("gy") * width_z
    source = sensitivity * probes.astype(jnp.float32)
    kpad = padded_2(permeability, (("gx", 0), ("gy", 1)), 1)
    coefs, diag = face_terms(kpad, absorption)
    forward = single_solve(source, coefs, diag)
    adjoint = single_solve(observe_weight * forward, coefs, diag)
    responses = (sensitivity * adjoint).reshape(count, -1)
    gram = jnp.dot(
        responses, responses.T, precision=lax.Precision.HIGHEST, preferred_element_type=jnp.float32
    ) / float(total_cells)
    summed = lax.psum(gram, ("gx", "gy"))
    r_factor = jnp.linalg.cholesky(summed).T
    inverse = lower_inverse(r_factor.T)
    q_basis = jnp.dot(
        inverse, responses, precision=lax.Precision.HIGHEST, preferred_element_type=jnp.float32
    )
    return (q_basis.reshape(count, width_x, width_y, width_z), r_factor)


def solution(mesh):
    return jax.shard_map(
        body,
        mesh=mesh,
        in_specs=(
            P(None, "gx", "gy", None),
            P("gx", "gy", None),
            P("gx", "gy", None),
            P("gx", "gy", None),
            P("gx", "gy", None),
        ),
        out_specs=(P(None, "gx", "gy", None), P()),
        check_vma=False,
    )
```

profile of v0, /device:TPU:1, one launch (start us, length us, event | category | flops | bytes accessed | tf_op | source)
XLA Modules:
  0.0 477.7 jit_solution(5736251679478385338)
XLA Ops:
  1.3 4.4 collective-permute-start
  7.9 2.4 collective-permute-done.1
  10.3 5.0 %collective-permute-start.2 = (f32[10,1,128]{2,1,0:T(1,128)S(1)}, f32[10,1,128]{2,1,0:T(1,128)S(1)}, u32[]{:S(2)}, u32[]{:S(2)}) collective-permute-start(f32[10,1,128]{2,1,0:T(1,128)S(1)} %get-tuple-element.132), channel_id=1, source_target_pairs={{0,1},{1,2},{2,3},{3,4},{4,5},{5,6},{6,7},{8,9},{9,10},{10,11},{11... | collective-permute-start | bytes 15368 | tf_op jit(solution)/shard_map/ppermute | solution.py:16
  17.3 3.0 collective-permute-done.3
  21.4 3.4 multiply_divide_fusion.1
  24.9 3.7 collective-permute-start.4
  29.9 9.0 %collective-permute-done.4 = f32[64,1,16,128]{3,0,2,1:T(8,128)S(1)} collective-permute-done((f32[64,1,16,128]{3,0,2,1:T(8,128)S(1)}, f32[64,1,16,128]{3,0,2,1:T(8,128)S(1)}, u32[]{:S(2)}, u32[]{:S(2)}) %collective-permute-start.4) | collective-permute-done | bytes 524320 | tf_op jit(solution)/shard_map/ppermute | solution.py:16
  38.9 5.1 %collective-permute-done.5 = f32[64,1,16,128]{3,0,2,1:T(8,128)S(1)} collective-permute-done((f32[64,1,16,128]{3,0,2,1:T(8,128)S(1)}, f32[64,1,16,128]{3,0,2,1:T(8,128)S(1)}, u32[]{:S(2)}, u32[]{:S(2)}) %collective-permute-start.5) | collective-permute-done | bytes 524320 | tf_op jit(solution)/shard_map/ppermute | solution.py:17
  44.1 3.9 collective-permute-start.6
  52.0 4.4 collective-permute-done.7
  56.4 7.8 %fusion.10 = f32[64,8,16,128]{3,0,2,1:T(8,128)S(1)} fusion(f32[64,8,16,128]{3,0,2,1:T(8,128)S(1)} %multiply_divide_fusion.1, f32[64,10,1,128]{3,0,2,1:T(8,128)S(1)} %collective-permute-done.7, f32[64,1,16,128]{3,0,2,1:T(8,128)S(1)} %collective-permute-done.5, f32[64,1,16,128]{3,0,2,1:T(8,128)S(1)} %collective-permute-done.4, ...), kind=kLoop, calls=%fused_computation.23 | loop fusion | flops 27262976 | bytes 12713984 | tf_op jit(solution)/shard_map/add | solution.py:41
  64.3 4.9 %collective-permute-start.8 = (f32[64,1,16,128]{3,0,2,1:T(8,128)S(1)}, f32[64,1,16,128]{3,0,2,1:T(8,128)S(1)}, u32[]{:S(2)}, u32[]{:S(2)}) collective-permute-start(f32[64,1,16,128]{3,0,2,1:T(8,128)S(1)} %get-tuple-element.127), channel_id=1, source_target_pairs={{0,8},{8,16},{16,24},{24,32},{32,40},{40,48},{48,56},{56,64},{64,7... | collective-permute-start | bytes 1572872 | tf_op jit(solution)/shard_map/ppermute | solution.py:16
  70.5 6.0 %collective-permute-done.8 = f32[64,1,16,128]{3,0,2,1:T(8,128)S(1)} collective-permute-done((f32[64,1,16,128]{3,0,2,1:T(8,128)S(1)}, f32[64,1,16,128]{3,0,2,1:T(8,128)S(1)}, u32[]{:S(2)}, u32[]{:S(2)}) %collective-permute-start.8) | collective-permute-done | bytes 524320 | tf_op jit(solution)/shard_map/ppermute | solution.py:16
  76.5 4.4 collective-permute-done.9
  81.0 6.2 %collective-permute-start.10 = (f32[64,10,1,128]{3,0,2,1:T(8,128)S(1)}, f32[64,10,1,128]{3,0,2,1:T(8,128)S(1)}, u32[]{:S(2)}, u32[]{:S(2)}) collective-permute-start(f32[64,10,1,128]{3,0,2,1:T(8,128)S(1)} %get-tuple-element.115), channel_id=1, source_target_pairs={{0,1},{1,2},{2,3},{3,4},{4,5},{5,6},{6,7},{8,9},{9,10},{10,11},{11... | collective-permute-start | bytes 983048 | tf_op jit(solution)/shard_map/ppermute | solution.py:16
  91.2 4.4 collective-permute-done.11
  95.6 7.8 %fusion.18 = f32[64,8,16,128]{3,0,2,1:T(8,128)S(1)} fusion(f32[64,8,16,128]{3,0,2,1:T(8,128)S(1)} %fusion.10, f32[64,10,1,128]{3,0,2,1:T(8,128)S(1)} %collective-permute-done.11, f32[64,1,16,128]{3,0,2,1:T(8,128)S(1)} %collective-permute-done.9, f32[64,1,16,128]{3,0,2,1:T(8,128)S(1)} %collective-permute-done.8, ...), kind=kLoop, calls=%fused_computation.31 | loop fusion | flops 27262976 | bytes 12713984 | tf_op jit(solution)/shard_map/add | solution.py:41
  103.5 4.0 collective-permute-start.12
  108.8 6.0 %collective-permute-done.12 = f32[64,1,16,128]{3,0,2,1:T(8,128)S(1)} collective-permute-done((f32[64,1,16,128]{3,0,2,1:T(8,128)S(1)}, f32[64,1,16,128]{3,0,2,1:T(8,128)S(1)}, u32[]{:S(2)}, u32[]{:S(2)}) %collective-permute-start.12) | collective-permute-done | bytes 524320 | tf_op jit(solution)/shard_map/ppermute | solution.py:16
  114.8 4.1 collective-permute-done.13
  119.0 6.7 %collective-permute-start.14 = (f32[64,10,1,128]{3,0,2,1:T(8,128)S(1)}, f32[64,10,1,128]{3,0,2,1:T(8,128)S(1)}, u32[]{:S(2)}, u32[]{:S(2)}) collective-permute-start(f32[64,10,1,128]{3,0,2,1:T(8,128)S(1)} %get-tuple-element.113), channel_id=1, source_target_pairs={{0,1},{1,2},{2,3},{3,4},{4,5},{5,6},{6,7},{8,9},{9,10},{10,11},{11... | collective-permute-start | bytes 983048 | tf_op jit(solution)/shard_map/ppermute | solution.py:16
  129.7 4.4 collective-permute-done.15
  134.1 7.9 %multiply_divide_fusion = (f32[64,8,16,128]{3,0,2,1:T(8,128)S(1)}, f32[64,8,16,128]{3,0,2,1:T(8,128)S(1)}) fusion(f32[8,16,128]{2,1,0:T(8,128)S(1)} %get-tuple-element.100, f32[8,16,128]{2,1,0:T(8,128)S(1)} %get-tuple-element.106, f32[64,8,16,128]{3,0,2,1:T(8,128)S(1)} %fusion.18, f32[8,16,128]{2,1,0:T(8,128)S(1)} %get-tuple-element.105, ...), kind=kLoop, calls=%fused_computation.158 | loop fusion | flops 30408704 | bytes 16973824 | tf_op jit(solution)/shard_map/div | solution.py:45
  145.5 6.0 %collective-permute-done.16 = f32[64,1,16,128]{3,0,2,1:T(8,128)S(1)} collective-permute-done((f32[64,1,16,128]{3,0,2,1:T(8,128)S(1)}, f32[64,1,16,128]{3,0,2,1:T(8,128)S(1)}, u32[]{:S(2)}, u32[]{:S(2)}) %collective-permute-start.16) | collective-permute-done | bytes 524320 | tf_op jit(solution)/shard_map/ppermute | solution.py:16
  151.5 4.1 collective-permute-done.17
  155.7 7.3 %collective-permute-start.18 = (f32[64,10,1,128]{3,0,2,1:T(8,128)S(1)}, f32[64,10,1,128]{3,0,2,1:T(8,128)S(1)}, u32[]{:S(2)}, u32[]{:S(2)}) collective-permute-start(f32[64,10,1,128]{3,0,2,1:T(8,128)S(1)} %get-tuple-element.111), channel_id=1, source_target_pairs={{0,1},{1,2},{2,3},{3,4},{4,5},{5,6},{6,7},{8,9},{9,10},{10,11},{11... | collective-permute-start | bytes 983048 | tf_op jit(solution)/shard_map/ppermute | solution.py:16
  163.0 2.4 collective-permute-start.19
  167.0 4.4 collective-permute-done.19
  171.4 13.2 %fusion.34 = f32[64,8,16,128]{3,0,2,1:T(8,128)S(1)} fusion(f32[64,8,16,128]{3,0,2,1:T(8,128)S(1)} %get-tuple-element.99, f32[64,8,16,128]{3,0,2,1:T(8,128)} %copy-done.4, f32[64,10,1,128]{3,0,2,1:T(8,128)S(1)} %collective-permute-done.19, f32[64,1,16,128]{3,0,2,1:T(8,128)S(1)} %collective-permute-done.17, f32[64,1,16,128]{3,0,2,1:T(8,128)S(1)} %collective-permute-done.16, ...), kind=kLoop, calls=%fused_computation.47 | loop fusion | flops 25165824 | bytes 14745600 | tf_op jit(solution)/shard_map/add | solution.py:41
  187.3 5.9 %collective-permute-done.20 = f32[64,1,16,128]{3,0,2,1:T(8,128)S(1)} collective-permute-done((f32[64,1,16,128]{3,0,2,1:T(8,128)S(1)}, f32[64,1,16,128]{3,0,2,1:T(8,128)S(1)}, u32[]{:S(2)}, u32[]{:S(2)}) %collective-permute-start.20) | collective-permute-done | bytes 524320 | tf_op jit(solution)/shard_map/ppermute | solution.py:16
  193.2 4.1 collective-permute-done.21
  197.4 6.9 %collective-permute-start.22 = (f32[64,10,1,128]{3,0,2,1:T(8,128)S(1)}, f32[64,10,1,128]{3,0,2,1:T(8,128)S(1)}, u32[]{:S(2)}, u32[]{:S(2)}) collective-permute-start(f32[64,10,1,128]{3,0,2,1:T(8,128)S(1)} %get-tuple-element.109), channel_id=1, source_target_pairs={{0,1},{1,2},{2,3},{3,4},{4,5},{5,6},{6,7},{8,9},{9,10},{10,11},{11... | collective-permute-start | bytes 983048 | tf_op jit(solution)/shard_map/ppermute | solution.py:16
  208.3 4.4 collective-permute-done.23
  212.7 13.2 %fusion.42 = f32[64,8,16,128]{3,0,2,1:T(8,128)S(1)} fusion(f32[64,8,16,128]{3,0,2,1:T(8,128)S(1)} %get-tuple-element.99, f32[64,8,16,128]{3,0,2,1:T(8,128)} %copy-done.3, f32[64,10,1,128]{3,0,2,1:T(8,128)S(1)} %collective-permute-done.23, f32[64,1,16,128]{3,0,2,1:T(8,128)S(1)} %collective-permute-done.21, f32[64,1,16,128]{3,0,2,1:T(8,128)S(1)} %collective-permute-done.20, ...), kind=kLoop, calls=%fused_computation.55 | loop fusion | flops 25165824 | bytes 14745600 | tf_op jit(solution)/shard_map/add | solution.py:41
  226.0 3.5 collective-permute-start.24
  230.8 6.0 %collective-permute-done.24 = f32[64,1,16,128]{3,0,2,1:T(8,128)S(1)} collective-permute-done((f32[64,1,16,128]{3,0,2,1:T(8,128)S(1)}, f32[64,1,16,128]{3,0,2,1:T(8,128)S(1)}, u32[]{:S(2)}, u32[]{:S(2)}) %collective-permute-start.24) | collective-permute-done | bytes 524320 | tf_op jit(solution)/shard_map/ppermute | solution.py:16
  236.8 4.1 collective-permute-done.25
  241.0 6.0 %collective-permute-start.26 = (f32[64,10,1,128]{3,0,2,1:T(8,128)S(1)}, f32[64,10,1,128]{3,0,2,1:T(8,128)S(1)}, u32[]{:S(2)}, u32[]{:S(2)}) collective-permute-start(f32[64,10,1,128]{3,0,2,1:T(8,128)S(1)} %get-tuple-element.107), channel_id=1, source_target_pairs={{0,1},{1,2},{2,3},{3,4},{4,5},{5,6},{6,7},{8,9},{9,10},{10,11},{11... | collective-permute-start | bytes 983048 | tf_op jit(solution)/shard_map/ppermute | solution.py:16
  251.0 4.4 collective-permute-done.27
  255.4 14.5 %fusion.97 = f32[64,8,16,128]{3,0,2,1:T(8,128)S(1)} fusion(f32[64,8,16,128]{3,0,2,1:T(8,128)} %copy-done, f32[64,8,16,128]{3,0,2,1:T(8,128)} %copy-done.2, f32[64,10,1,128]{3,0,2,1:T(8,128)S(1)} %collective-permute-done.27, f32[64,1,16,128]{3,0,2,1:T(8,128)S(1)} %collective-permute-done.25, f32[64,1,16,128]{3,0,2,1:T(8,128)S(1)} %collective-permute-done.24, ...), kind=kLoop, calls=%fused_computation.162 | loop fusion | flops 26214400 | bytes 14811136 | tf_op jit(solution)/shard_map/mul | solution.py:77
  271.9 3.4 fusion.98
  275.3 80.6 %psum.7 = f32[64,64]{0,1:T(8,128)S(1)} all-reduce(f32[64,64]{0,1:T(8,128)S(1)} %fusion.98), channel_id=1, replica_groups=mesh['gx'=32,'gy'=8] {'gx','gy'}, use_global_device_ids=true, to_apply=%region_0.1 | all-reduce | flops 4096 | bytes 32768 | tf_op jit(solution)/shard_map/psum | solution.py:81
  356.0 5.8 %cholesky.19 = f32[64,64]{1,0:T(8,128)S(1)} custom-call(f32[64,64]{1,0:T(8,128)S(1)} %fusion.112), custom_call_target="Cholesky" | custom-call | tf_op jit(solution)/shard_map/jit(cholesky)/cholesky | solution.py:82
  363.9 6.6 %copy.29 = f32[64,8,16,128]{3,2,1,0:T(8,128)} copy(f32[64,8,16,128]{3,0,2,1:T(8,128)} %copy-done.1) | data formatting | bytes 8388608 | tf_op jit(solution)/shard_map/mul | solution.py:77
  371.2 90.6 %while.13 = (s32[]{:T(128)}, f32[64,64]{1,0:T(8,128)S(1)}, f32[64,64]{1,0:T(8,128)S(1)}, f32[64,64]{1,0:T(8,128)S(1)}, s32[]{:T(128)}, /*index=5*/s32[]{:T(128)}) while((s32[]{:T(128)}, f32[64,64]{1,0:T(8,128)S(1)}, f32[64,64]{1,0:T(8,128)S(1)}, f32[64,64]{1,0:T(8,128)S(1)}, s32[]{:T(128)}, /*index=5*/s32[]{:T(128)}) %tuple.57), condition=%wide.region_4.5_spmd, body=%wide.region_3.4_spmd.sunk | while | flops 49282 | bytes 36181 | solution.py:66
  461.7 4.6 copy.46
  467.1 6.0 %fusion.94 = f32[64,8,16,128]{3,0,2,1:T(8,128)S(1)} fusion(f32[8,16,128,64]{2,1,0,3:T(8,128)S(1)} %bitcast.44, f32[64,64]{1,0:T(8,128)S(1)} %get-tuple-element.81), kind=kOutput, calls=%fused_computation.156 | convolution fusion | flops 805306368 | bytes 8404992 | tf_op jit(solution)/shard_map/dot_general | solution.py:84
  473.0 4.4 copy.31
  (259 shorter events, 134.3 us)
Async XLA Ops:
  1.3 5.7 %collective-permute-start = (f32[1,16,128]{2,1,0:T(8,128)S(1)}, f32[1,16,128]{2,1,0:T(8,128)S(1)}, u32[]{:S(2)}, u32[]{:S(2)}) collective-permute-start(f32[1,16,128]{2,1,0:T(8,128)S(1)} %get-tuple-element.134), channel_id=1, source_target_pairs={{0,8},{8,16},{16,24},{24,32},{32,40},{40,48},{48,56},{56,64},{64,7... | collective-permute-start | bytes 24584 | tf_op jit(solution)/shard_map/ppermute | solution.py:16
  5.7 4.6 collective-permute-start.1
  10.3 6.9 %collective-permute-start.2 = (f32[10,1,128]{2,1,0:T(1,128)S(1)}, f32[10,1,128]{2,1,0:T(1,128)S(1)}, u32[]{:S(2)}, u32[]{:S(2)}) collective-permute-start(f32[10,1,128]{2,1,0:T(1,128)S(1)} %get-tuple-element.132), channel_id=1, source_target_pairs={{0,1},{1,2},{2,3},{3,4},{4,5},{5,6},{6,7},{8,9},{9,10},{10,11},{11... | collective-permute-start | bytes 15368 | tf_op jit(solution)/shard_map/ppermute | solution.py:16
  15.3 4.9 %collective-permute-start.3 = (f32[10,1,128]{2,1,0:T(1,128)S(1)}, f32[10,1,128]{2,1,0:T(1,128)S(1)}, u32[]{:S(2)}, u32[]{:S(2)}) collective-permute-start(f32[10,1,128]{2,1,0:T(1,128)S(1)} %get-tuple-element.131), channel_id=1, source_target_pairs={{1,0},{2,1},{3,2},{4,3},{5,4},{6,5},{7,6},{9,8},{10,9},{11,10},{12... | collective-permute-start | bytes 15368 | tf_op jit(solution)/shard_map/ppermute | solution.py:17
  24.8 31.6 %copy-start.5 = (bf16[64,8,16,128]{3,2,1,0:T(8,128)(2,1)S(1)}, bf16[64,8,16,128]{3,2,1,0:T(8,128)(2,1)}, u32[]{:S(2)}) copy-start(bf16[64,8,16,128]{3,2,1,0:T(8,128)(2,1)} %param.7) | copy-start | bytes 6291460
  24.8 31.6 %copy-start.6 = (f32[8,16,128]{2,1,0:T(8,128)S(1)}, f32[8,16,128]{2,1,0:T(8,128)}, u32[]{:S(2)}) copy-start(f32[8,16,128]{2,1,0:T(8,128)} %param.10) | copy-start | bytes 196612
  24.9 14.0 %collective-permute-start.4 = (f32[64,1,16,128]{3,0,2,1:T(8,128)S(1)}, f32[64,1,16,128]{3,0,2,1:T(8,128)S(1)}, u32[]{:S(2)}, u32[]{:S(2)}) collective-permute-start(f32[64,1,16,128]{3,0,2,1:T(8,128)S(1)} %get-tuple-element.129), channel_id=1, source_target_pairs={{0,8},{8,16},{16,24},{24,32},{32,40},{40,48},{48,56},{56,64},{64,7... | collective-permute-start | bytes 1572872 | tf_op jit(solution)/shard_map/ppermute | solution.py:16
  28.6 15.4 %collective-permute-start.5 = (f32[64,1,16,128]{3,0,2,1:T(8,128)S(1)}, f32[64,1,16,128]{3,0,2,1:T(8,128)S(1)}, u32[]{:S(2)}, u32[]{:S(2)}) collective-permute-start(f32[64,1,16,128]{3,0,2,1:T(8,128)S(1)} %get-tuple-element.130), channel_id=1, source_target_pairs={{8,0},{16,8},{24,16},{32,24},{40,32},{48,40},{56,48},{64,56},{72,6... | collective-permute-start | bytes 1572872 | tf_op jit(solution)/shard_map/ppermute | solution.py:17
  44.1 7.9 %collective-permute-start.6 = (f32[64,10,1,128]{3,0,2,1:T(8,128)S(1)}, f32[64,10,1,128]{3,0,2,1:T(8,128)S(1)}, u32[]{:S(2)}, u32[]{:S(2)}) collective-permute-start(f32[64,10,1,128]{3,0,2,1:T(8,128)S(1)} %get-tuple-element.117), channel_id=1, source_target_pairs={{0,1},{1,2},{2,3},{3,4},{4,5},{5,6},{6,7},{8,9},{9,10},{10,11},{11... | collective-permute-start | bytes 983048 | tf_op jit(solution)/shard_map/ppermute | solution.py:16
  48.0 8.4 %collective-permute-start.7 = (f32[64,10,1,128]{3,0,2,1:T(8,128)S(1)}, f32[64,10,1,128]{3,0,2,1:T(8,128)S(1)}, u32[]{:S(2)}, u32[]{:S(2)}) collective-permute-start(f32[64,10,1,128]{3,0,2,1:T(8,128)S(1)} %get-tuple-element.118), channel_id=1, source_target_pairs={{1,0},{2,1},{3,2},{4,3},{5,4},{6,5},{7,6},{9,8},{10,9},{11,10},{12... | collective-permute-start | bytes 983048 | tf_op jit(solution)/shard_map/ppermute | solution.py:17
  64.3 12.2 %collective-permute-start.8 = (f32[64,1,16,128]{3,0,2,1:T(8,128)S(1)}, f32[64,1,16,128]{3,0,2,1:T(8,128)S(1)}, u32[]{:S(2)}, u32[]{:S(2)}) collective-permute-start(f32[64,1,16,128]{3,0,2,1:T(8,128)S(1)} %get-tuple-element.127), channel_id=1, source_target_pairs={{0,8},{8,16},{16,24},{24,32},{32,40},{40,48},{48,56},{56,64},{64,7... | collective-permute-start | bytes 1572872 | tf_op jit(solution)/shard_map/ppermute | solution.py:16
  69.2 11.7 %collective-permute-start.9 = (f32[64,1,16,128]{3,0,2,1:T(8,128)S(1)}, f32[64,1,16,128]{3,0,2,1:T(8,128)S(1)}, u32[]{:S(2)}, u32[]{:S(2)}) collective-permute-start(f32[64,1,16,128]{3,0,2,1:T(8,128)S(1)} %get-tuple-element.128), channel_id=1, source_target_pairs={{8,0},{16,8},{24,16},{32,24},{40,32},{48,40},{56,48},{64,56},{72,6... | collective-permute-start | bytes 1572872 | tf_op jit(solution)/shard_map/ppermute | solution.py:17
  81.0 10.2 %collective-permute-start.10 = (f32[64,10,1,128]{3,0,2,1:T(8,128)S(1)}, f32[64,10,1,128]{3,0,2,1:T(8,128)S(1)}, u32[]{:S(2)}, u32[]{:S(2)}) collective-permute-start(f32[64,10,1,128]{3,0,2,1:T(8,128)S(1)} %get-tuple-element.115), channel_id=1, source_target_pairs={{0,1},{1,2},{2,3},{3,4},{4,5},{5,6},{6,7},{8,9},{9,10},{10,11},{11... | collective-permute-start | bytes 983048 | tf_op jit(solution)/shard_map/ppermute | solution.py:16
  87.2 8.4 %collective-permute-start.11 = (f32[64,10,1,128]{3,0,2,1:T(8,128)S(1)}, f32[64,10,1,128]{3,0,2,1:T(8,128)S(1)}, u32[]{:S(2)}, u32[]{:S(2)}) collective-permute-start(f32[64,10,1,128]{3,0,2,1:T(8,128)S(1)} %get-tuple-element.116), channel_id=1, source_target_pairs={{1,0},{2,1},{3,2},{4,3},{5,4},{6,5},{7,6},{9,8},{10,9},{11,10},{12... | collective-permute-start | bytes 983048 | tf_op jit(solution)/shard_map/ppermute | solution.py:17
  103.4 30.7 %copy-start.7 = (f32[8,16,128]{2,1,0:T(8,128)S(1)}, f32[8,16,128]{2,1,0:T(8,128)}, u32[]{:S(2)}) copy-start(f32[8,16,128]{2,1,0:T(8,128)} %param.11) | copy-start | bytes 196612
  103.5 11.3 %collective-permute-start.12 = (f32[64,1,16,128]{3,0,2,1:T(8,128)S(1)}, f32[64,1,16,128]{3,0,2,1:T(8,128)S(1)}, u32[]{:S(2)}, u32[]{:S(2)}) collective-permute-start(f32[64,1,16,128]{3,0,2,1:T(8,128)S(1)} %get-tuple-element.125), channel_id=1, source_target_pairs={{0,8},{8,16},{16,24},{24,32},{32,40},{40,48},{48,56},{56,64},{64,7... | collective-permute-start | bytes 1572872 | tf_op jit(solution)/shard_map/ppermute | solution.py:16
  107.5 11.4 %collective-permute-start.13 = (f32[64,1,16,128]{3,0,2,1:T(8,128)S(1)}, f32[64,1,16,128]{3,0,2,1:T(8,128)S(1)}, u32[]{:S(2)}, u32[]{:S(2)}) collective-permute-start(f32[64,1,16,128]{3,0,2,1:T(8,128)S(1)} %get-tuple-element.126), channel_id=1, source_target_pairs={{8,0},{16,8},{24,16},{32,24},{40,32},{48,40},{56,48},{64,56},{72,6... | collective-permute-start | bytes 1572872 | tf_op jit(solution)/shard_map/ppermute | solution.py:17
  119.0 10.7 %collective-permute-start.14 = (f32[64,10,1,128]{3,0,2,1:T(8,128)S(1)}, f32[64,10,1,128]{3,0,2,1:T(8,128)S(1)}, u32[]{:S(2)}, u32[]{:S(2)}) collective-permute-start(f32[64,10,1,128]{3,0,2,1:T(8,128)S(1)} %get-tuple-element.113), channel_id=1, source_target_pairs={{0,1},{1,2},{2,3},{3,4},{4,5},{5,6},{6,7},{8,9},{9,10},{10,11},{11... | collective-permute-start | bytes 983048 | tf_op jit(solution)/shard_map/ppermute | solution.py:16
  125.7 8.4 %collective-permute-start.15 = (f32[64,10,1,128]{3,0,2,1:T(8,128)S(1)}, f32[64,10,1,128]{3,0,2,1:T(8,128)S(1)}, u32[]{:S(2)}, u32[]{:S(2)}) collective-permute-start(f32[64,10,1,128]{3,0,2,1:T(8,128)S(1)} %get-tuple-element.114), channel_id=1, source_target_pairs={{1,0},{2,1},{3,2},{4,3},{5,4},{6,5},{7,6},{9,8},{10,9},{11,10},{12... | collective-permute-start | bytes 983048 | tf_op jit(solution)/shard_map/ppermute | solution.py:17
  142.0 29.3 %copy-start.4 = (f32[64,8,16,128]{3,0,2,1:T(8,128)}, f32[64,8,16,128]{3,0,2,1:T(8,128)S(1)}, u32[]{:S(2)}) copy-start(f32[64,8,16,128]{3,0,2,1:T(8,128)S(1)} %get-tuple-element.98) | copy-start | bytes 12582916
  142.1 70.7 %copy-start = (f32[64,8,16,128]{3,0,2,1:T(8,128)}, f32[64,8,16,128]{3,0,2,1:T(8,128)S(1)}, u32[]{:S(2)}) copy-start(f32[64,8,16,128]{3,0,2,1:T(8,128)S(1)} %get-tuple-element.99) | copy-start | bytes 12582916
  142.1 9.4 %collective-permute-start.16 = (f32[64,1,16,128]{3,0,2,1:T(8,128)S(1)}, f32[64,1,16,128]{3,0,2,1:T(8,128)S(1)}, u32[]{:S(2)}, u32[]{:S(2)}) collective-permute-start(f32[64,1,16,128]{3,0,2,1:T(8,128)S(1)} %get-tuple-element.123), channel_id=1, source_target_pairs={{0,8},{8,16},{16,24},{24,32},{32,40},{40,48},{48,56},{56,64},{64,7... | collective-permute-start | bytes 1572872 | tf_op jit(solution)/shard_map/ppermute | solution.py:16
  144.2 11.4 %collective-permute-start.17 = (f32[64,1,16,128]{3,0,2,1:T(8,128)S(1)}, f32[64,1,16,128]{3,0,2,1:T(8,128)S(1)}, u32[]{:S(2)}, u32[]{:S(2)}) collective-permute-start(f32[64,1,16,128]{3,0,2,1:T(8,128)S(1)} %get-tuple-element.124), channel_id=1, source_target_pairs={{8,0},{16,8},{24,16},{32,24},{40,32},{48,40},{56,48},{64,56},{72,6... | collective-permute-start | bytes 1572872 | tf_op jit(solution)/shard_map/ppermute | solution.py:17
  155.7 11.3 %collective-permute-start.18 = (f32[64,10,1,128]{3,0,2,1:T(8,128)S(1)}, f32[64,10,1,128]{3,0,2,1:T(8,128)S(1)}, u32[]{:S(2)}, u32[]{:S(2)}) collective-permute-start(f32[64,10,1,128]{3,0,2,1:T(8,128)S(1)} %get-tuple-element.111), channel_id=1, source_target_pairs={{0,1},{1,2},{2,3},{3,4},{4,5},{5,6},{6,7},{8,9},{9,10},{10,11},{11... | collective-permute-start | bytes 983048 | tf_op jit(solution)/shard_map/ppermute | solution.py:16
  163.0 8.4 %collective-permute-start.19 = (f32[64,10,1,128]{3,0,2,1:T(8,128)S(1)}, f32[64,10,1,128]{3,0,2,1:T(8,128)S(1)}, u32[]{:S(2)}, u32[]{:S(2)}) collective-permute-start(f32[64,10,1,128]{3,0,2,1:T(8,128)S(1)} %get-tuple-element.112), channel_id=1, source_target_pairs={{1,0},{2,1},{3,2},{4,3},{5,4},{6,5},{7,6},{9,8},{10,9},{11,10},{12... | collective-permute-start | bytes 983048 | tf_op jit(solution)/shard_map/ppermute | solution.py:17
  184.6 23.7 %copy-start.3 = (f32[64,8,16,128]{3,0,2,1:T(8,128)}, f32[64,8,16,128]{3,0,2,1:T(8,128)S(1)}, u32[]{:S(2)}) copy-start(f32[64,8,16,128]{3,0,2,1:T(8,128)S(1)} %fusion.34) | copy-start | bytes 12582916
  184.7 8.5 %collective-permute-start.20 = (f32[64,1,16,128]{3,0,2,1:T(8,128)S(1)}, f32[64,1,16,128]{3,0,2,1:T(8,128)S(1)}, u32[]{:S(2)}, u32[]{:S(2)}) collective-permute-start(f32[64,1,16,128]{3,0,2,1:T(8,128)S(1)} %get-tuple-element.121), channel_id=1, source_target_pairs={{0,8},{8,16},{16,24},{24,32},{32,40},{40,48},{48,56},{56,64},{64,7... | collective-permute-start | bytes 1572872 | tf_op jit(solution)/shard_map/ppermute | solution.py:16
  186.0 11.3 %collective-permute-start.21 = (f32[64,1,16,128]{3,0,2,1:T(8,128)S(1)}, f32[64,1,16,128]{3,0,2,1:T(8,128)S(1)}, u32[]{:S(2)}, u32[]{:S(2)}) collective-permute-start(f32[64,1,16,128]{3,0,2,1:T(8,128)S(1)} %get-tuple-element.122), channel_id=1, source_target_pairs={{8,0},{16,8},{24,16},{32,24},{40,32},{48,40},{56,48},{64,56},{72,6... | collective-permute-start | bytes 1572872 | tf_op jit(solution)/shard_map/ppermute | solution.py:17
  197.4 10.9 %collective-permute-start.22 = (f32[64,10,1,128]{3,0,2,1:T(8,128)S(1)}, f32[64,10,1,128]{3,0,2,1:T(8,128)S(1)}, u32[]{:S(2)}, u32[]{:S(2)}) collective-permute-start(f32[64,10,1,128]{3,0,2,1:T(8,128)S(1)} %get-tuple-element.109), channel_id=1, source_target_pairs={{0,1},{1,2},{2,3},{3,4},{4,5},{5,6},{6,7},{8,9},{9,10},{10,11},{11... | collective-permute-start | bytes 983048 | tf_op jit(solution)/shard_map/ppermute | solution.py:16
  204.3 8.4 %collective-permute-start.23 = (f32[64,10,1,128]{3,0,2,1:T(8,128)S(1)}, f32[64,10,1,128]{3,0,2,1:T(8,128)S(1)}, u32[]{:S(2)}, u32[]{:S(2)}) collective-permute-start(f32[64,10,1,128]{3,0,2,1:T(8,128)S(1)} %get-tuple-element.110), channel_id=1, source_target_pairs={{1,0},{2,1},{3,2},{4,3},{5,4},{6,5},{7,6},{9,8},{10,9},{11,10},{12... | collective-permute-start | bytes 983048 | tf_op jit(solution)/shard_map/ppermute | solution.py:17
  225.9 15.0 %copy-start.2 = (f32[64,8,16,128]{3,0,2,1:T(8,128)}, f32[64,8,16,128]{3,0,2,1:T(8,128)S(1)}, u32[]{:S(2)}) copy-start(f32[64,8,16,128]{3,0,2,1:T(8,128)S(1)} %fusion.42) | copy-start | bytes 12582916
  226.0 10.8 %collective-permute-start.24 = (f32[64,1,16,128]{3,0,2,1:T(8,128)S(1)}, f32[64,1,16,128]{3,0,2,1:T(8,128)S(1)}, u32[]{:S(2)}, u32[]{:S(2)}) collective-permute-start(f32[64,1,16,128]{3,0,2,1:T(8,128)S(1)} %get-tuple-element.119), channel_id=1, source_target_pairs={{0,8},{8,16},{16,24},{24,32},{32,40},{40,48},{48,56},{56,64},{64,7... | collective-permute-start | bytes 1572872 | tf_op jit(solution)/shard_map/ppermute | solution.py:16
  229.5 11.4 %collective-permute-start.25 = (f32[64,1,16,128]{3,0,2,1:T(8,128)S(1)}, f32[64,1,16,128]{3,0,2,1:T(8,128)S(1)}, u32[]{:S(2)}, u32[]{:S(2)}) collective-permute-start(f32[64,1,16,128]{3,0,2,1:T(8,128)S(1)} %get-tuple-element.120), channel_id=1, source_target_pairs={{8,0},{16,8},{24,16},{32,24},{40,32},{48,40},{56,48},{64,56},{72,6... | collective-permute-start | bytes 1572872 | tf_op jit(solution)/shard_map/ppermute | solution.py:17
  241.0 10.0 %collective-permute-start.26 = (f32[64,10,1,128]{3,0,2,1:T(8,128)S(1)}, f32[64,10,1,128]{3,0,2,1:T(8,128)S(1)}, u32[]{:S(2)}, u32[]{:S(2)}) collective-permute-start(f32[64,10,1,128]{3,0,2,1:T(8,128)S(1)} %get-tuple-element.107), channel_id=1, source_target_pairs={{0,1},{1,2},{2,3},{3,4},{4,5},{5,6},{6,7},{8,9},{9,10},{10,11},{11... | collective-permute-start | bytes 983048 | tf_op jit(solution)/shard_map/ppermute | solution.py:16
  247.0 8.4 %collective-permute-start.27 = (f32[64,10,1,128]{3,0,2,1:T(8,128)S(1)}, f32[64,10,1,128]{3,0,2,1:T(8,128)S(1)}, u32[]{:S(2)}, u32[]{:S(2)}) collective-permute-start(f32[64,10,1,128]{3,0,2,1:T(8,128)S(1)} %get-tuple-element.108), channel_id=1, source_target_pairs={{1,0},{2,1},{3,2},{4,3},{5,4},{6,5},{7,6},{9,8},{10,9},{11,10},{12... | collective-permute-start | bytes 983048 | tf_op jit(solution)/shard_map/ppermute | solution.py:17
  269.9 2.0 copy-start.1
where the time goes:
time: 487 us; the launch traced here: 478 us
  waiting for transfers between devices  108 us (22%)
  starting transfers between devices  88.9 us (18%)
  blocking collectives  80.6 us (17%)
  other arithmetic  77.1 us (16%)
  local copies, waits for them, and re-layouts  60.6 us (12%)
  matrix products  59.3 us (12%)
    psum x1, blocking collectives, body(): summed = lax.psum(gram, ('gx', 'gy'))  80.6 us
    ppermute x14, starting transfers between devices, padded_2(): before = lax.ppermute(last, axis, up)  65.8 us
    ppermute x14, waiting for transfers between devices, padded_2(): after = lax.ppermute(first, axis, down)  57.8 us
    ppermute x14, waiting for transfers between devices, padded_2(): before = lax.ppermute(last, axis, up)  50.6 us
    dot_general x64, matrix products, row_step(): jnp.dot(row, inverse, precision=lax.Precision.HIGHEST, preferred_element_...  50 us
    add x4, other arithmetic, sweep(): return 0.2 * field + 0.8 * (rhs + total) / diag  42 us
    dynamic_slice x64, local copies, waits for them, and re-layouts, row_step(): pivot = lax.dynamic_slice(lower, (index, index), (1, 1))  37.6 us
    ppermute x14, starting transfers between devices, padded_2(): after = lax.ppermute(first, axis, down)  23.1 us
  transfers between devices with their start and end apart: 28, of which 26 were waited for; matrix products, arithmetic and copies ran while one was open for 0% of the time, Pallas kernels for 0%

commit v1 on v0

--- a/solution.py
+++ b/solution.py
@@ -78,7 +78,7 @@
     gram = jnp.dot(
         responses, responses.T, precision=lax.Precision.HIGHEST, preferred_element_type=jnp.float32
     ) / float(total_cells)
-    summed = lax.psum(gram, ("gx", "gy"))
+    summed = lax.psum(lax.psum(gram, "gx"), "gy")
     r_factor = jnp.linalg.cholesky(summed).T
     inverse = lower_inverse(r_factor.T)
     q_basis = jnp.dot(

time: 487 us -> 563 us (1.16)
  blocking collectives: 80.6 us -> 157 us
    psum x1 -> x2, blocking collectives: 80.6 us -> 157 us  [body(): summed = lax.psum(lax.psum(gram, 'gx'), 'gy')]
where the time goes in v1:
time: 563 us; the launch traced here: 553 us
  blocking collectives  157 us (28%)
  waiting for transfers between devices  108 us (19%)
  starting transfers between devices  88.9 us (16%)
  other arithmetic  77 us (14%)
  local copies, waits for them, and re-layouts  60.6 us (11%)
  matrix products  59.3 us (11%)
    psum x2, blocking collectives, body(): summed = lax.psum(lax.psum(gram, 'gx'), 'gy')  157 us
    ppermute x14, starting transfers between devices, padded_2(): before = lax.ppermute(last, axis, up)  65.8 us
    ppermute x14, waiting for transfers between devices, padded_2(): after = lax.ppermute(first, axis, down)  57.8 us
    ppermute x14, waiting for transfers between devices, padded_2(): before = lax.ppermute(last, axis, up)  50.6 us
    dot_general x64, matrix products, row_step(): jnp.dot(row, inverse, precision=lax.Precision.HIGHEST, preferred_element_...  50 us
    add x4, other arithmetic, sweep(): return 0.2 * field + 0.8 * (rhs + total) / diag  41.9 us
    dynamic_slice x64, local copies, waits for them, and re-layouts, row_step(): pivot = lax.dynamic_slice(lower, (index, index), (1, 1))  37.6 us
    ppermute x14, starting transfers between devices, padded_2(): after = lax.ppermute(first, axis, down)  23.1 us
  transfers between devices with their start and end apart: 28, of which 26 were waited for; matrix products, arithmetic and copies ran while one was open for 0% of the time, Pallas kernels for 0%

profile of v1, /device:TPU:1, one launch (start us, length us, event | category | flops | bytes accessed | tf_op | source)
XLA Modules:
  0.0 553.5 jit_solution(13911498389129882194)
XLA Ops:
  1.3 4.4 collective-permute-start
  7.9 2.4 collective-permute-done.1
  10.3 5.0 collective-permute-start.2
  17.3 3.0 collective-permute-done.3
  21.4 3.4 multiply_divide_fusion.1
  24.9 3.7 collective-permute-start.4
  29.9 9.0 %collective-permute-done.4 = f32[64,1,16,128]{3,0,2,1:T(8,128)S(1)} collective-permute-done((f32[64,1,16,128]{3,0,2,1:T(8,128)S(1)}, f32[64,1,16,128]{3,0,2,1:T(8,128)S(1)}, u32[]{:S(2)}, u32[]{:S(2)}) %collective-permute-start.4) | collective-permute-done | bytes 524320 | tf_op jit(solution)/shard_map/ppermute | solution.py:16
  38.9 5.1 collective-permute-done.5
  44.1 3.9 collective-permute-start.6
  52.0 4.4 collective-permute-done.7
  56.4 7.8 %fusion.10 = f32[64,8,16,128]{3,0,2,1:T(8,128)S(1)} fusion(f32[64,8,16,128]{3,0,2,1:T(8,128)S(1)} %multiply_divide_fusion.1, f32[64,10,1,128]{3,0,2,1:T(8,128)S(1)} %collective-permute-done.7, f32[64,1,16,128]{3,0,2,1:T(8,128)S(1)} %collective-permute-done.5, f32[64,1,16,128]{3,0,2,1:T(8,128)S(1)} %collective-permute-done.4, ...), kind=kLoop, calls=%fused_computation.23 | loop fusion | flops 27262976 | bytes 12713984 | tf_op jit(solution)/shard_map/add | solution.py:41
  64.3 4.9 collective-permute-start.8
  70.5 6.0 %collective-permute-done.8 = f32[64,1,16,128]{3,0,2,1:T(8,128)S(1)} collective-permute-done((f32[64,1,16,128]{3,0,2,1:T(8,128)S(1)}, f32[64,1,16,128]{3,0,2,1:T(8,128)S(1)}, u32[]{:S(2)}, u32[]{:S(2)}) %collective-permute-start.8) | collective-permute-done | bytes 524320 | tf_op jit(solution)/shard_map/ppermute | solution.py:16
  76.5 4.4 collective-permute-done.9
  81.0 6.2 %collective-permute-start.10 = (f32[64,10,1,128]{3,0,2,1:T(8,128)S(1)}, f32[64,10,1,128]{3,0,2,1:T(8,128)S(1)}, u32[]{:S(2)}, u32[]{:S(2)}) collective-permute-start(f32[64,10,1,128]{3,0,2,1:T(8,128)S(1)} %get-tuple-element.115), channel_id=1, source_target_pairs={{0,1},{1,2},{2,3},{3,4},{4,5},{5,6},{6,7},{8,9},{9,10},{10,11},{11... | collective-permute-start | bytes 983048 | tf_op jit(solution)/shard_map/ppermute | solution.py:16
  91.2 4.4 collective-permute-done.11
  95.6 7.8 %fusion.18 = f32[64,8,16,128]{3,0,2,1:T(8,128)S(1)} fusion(f32[64,8,16,128]{3,0,2,1:T(8,128)S(1)} %fusion.10, f32[64,10,1,128]{3,0,2,1:T(8,128)S(1)} %collective-permute-done.11, f32[64,1,16,128]{3,0,2,1:T(8,128)S(1)} %collective-permute-done.9, f32[64,1,16,128]{3,0,2,1:T(8,128)S(1)} %collective-permute-done.8, ...), kind=kLoop, calls=%fused_computation.31 | loop fusion | flops 27262976 | bytes 12713984 | tf_op jit(solution)/shard_map/add | solution.py:41
  103.5 4.0 collective-permute-start.12
  108.8 6.0 %collective-permute-done.12 = f32[64,1,16,128]{3,0,2,1:T(8,128)S(1)} collective-permute-done((f32[64,1,16,128]{3,0,2,1:T(8,128)S(1)}, f32[64,1,16,128]{3,0,2,1:T(8,128)S(1)}, u32[]{:S(2)}, u32[]{:S(2)}) %collective-permute-start.12) | collective-permute-done | bytes 524320 | tf_op jit(solution)/shard_map/ppermute | solution.py:16
  114.8 4.1 collective-permute-done.13
  119.0 6.7 %collective-permute-start.14 = (f32[64,10,1,128]{3,0,2,1:T(8,128)S(1)}, f32[64,10,1,128]{3,0,2,1:T(8,128)S(1)}, u32[]{:S(2)}, u32[]{:S(2)}) collective-permute-start(f32[64,10,1,128]{3,0,2,1:T(8,128)S(1)} %get-tuple-element.113), channel_id=1, source_target_pairs={{0,1},{1,2},{2,3},{3,4},{4,5},{5,6},{6,7},{8,9},{9,10},{10,11},{11... | collective-permute-start | bytes 983048 | tf_op jit(solution)/shard_map/ppermute | solution.py:16
  129.7 4.4 collective-permute-done.15
  134.1 7.9 %multiply_divide_fusion = (f32[64,8,16,128]{3,0,2,1:T(8,128)S(1)}, f32[64,8,16,128]{3,0,2,1:T(8,128)S(1)}) fusion(f32[8,16,128]{2,1,0:T(8,128)S(1)} %get-tuple-element.100, f32[8,16,128]{2,1,0:T(8,128)S(1)} %get-tuple-element.106, f32[64,8,16,128]{3,0,2,1:T(8,128)S(1)} %fusion.18, f32[8,16,128]{2,1,0:T(8,128)S(1)} %get-tuple-element.105, ...), kind=kLoop, calls=%fused_computation.158 | loop fusion | flops 30408704 | bytes 16973824 | tf_op jit(solution)/shard_map/div | solution.py:45
  145.5 6.0 %collective-permute-done.16 = f32[64,1,16,128]{3,0,2,1:T(8,128)S(1)} collective-permute-done((f32[64,1,16,128]{3,0,2,1:T(8,128)S(1)}, f32[64,1,16,128]{3,0,2,1:T(8,128)S(1)}, u32[]{:S(2)}, u32[]{:S(2)}) %collective-permute-start.16) | collective-permute-done | bytes 524320 | tf_op jit(solution)/shard_map/ppermute | solution.py:16
  151.5 4.1 collective-permute-done.17
  155.7 7.3 %collective-permute-start.18 = (f32[64,10,1,128]{3,0,2,1:T(8,128)S(1)}, f32[64,10,1,128]{3,0,2,1:T(8,128)S(1)}, u32[]{:S(2)}, u32[]{:S(2)}) collective-permute-start(f32[64,10,1,128]{3,0,2,1:T(8,128)S(1)} %get-tuple-element.111), channel_id=1, source_target_pairs={{0,1},{1,2},{2,3},{3,4},{4,5},{5,6},{6,7},{8,9},{9,10},{10,11},{11... | collective-permute-start | bytes 983048 | tf_op jit(solution)/shard_map/ppermute | solution.py:16
  167.0 4.4 collective-permute-done.19
  171.4 13.1 %fusion.34 = f32[64,8,16,128]{3,0,2,1:T(8,128)S(1)} fusion(f32[64,8,16,128]{3,0,2,1:T(8,128)S(1)} %get-tuple-element.99, f32[64,8,16,128]{3,0,2,1:T(8,128)} %copy-done.4, f32[64,10,1,128]{3,0,2,1:T(8,128)S(1)} %collective-permute-done.19, f32[64,1,16,128]{3,0,2,1:T(8,128)S(1)} %collective-permute-done.17, f32[64,1,16,128]{3,0,2,1:T(8,128)S(1)} %collective-permute-done.16, ...), kind=kLoop, calls=%fused_computation.47 | loop fusion | flops 25165824 | bytes 14745600 | tf_op jit(solution)/shard_map/add | solution.py:41
  187.3 5.9 %collective-permute-done.20 = f32[64,1,16,128]{3,0,2,1:T(8,128)S(1)} collective-permute-done((f32[64,1,16,128]{3,0,2,1:T(8,128)S(1)}, f32[64,1,16,128]{3,0,2,1:T(8,128)S(1)}, u32[]{:S(2)}, u32[]{:S(2)}) %collective-permute-start.20) | collective-permute-done | bytes 524320 | tf_op jit(solution)/shard_map/ppermute | solution.py:16
  193.2 4.1 collective-permute-done.21
  197.4 6.9 %collective-permute-start.22 = (f32[64,10,1,128]{3,0,2,1:T(8,128)S(1)}, f32[64,10,1,128]{3,0,2,1:T(8,128)S(1)}, u32[]{:S(2)}, u32[]{:S(2)}) collective-permute-start(f32[64,10,1,128]{3,0,2,1:T(8,128)S(1)} %get-tuple-element.109), channel_id=1, source_target_pairs={{0,1},{1,2},{2,3},{3,4},{4,5},{5,6},{6,7},{8,9},{9,10},{10,11},{11... | collective-permute-start | bytes 983048 | tf_op jit(solution)/shard_map/ppermute | solution.py:16
  208.3 4.4 collective-permute-done.23
  212.7 13.1 %fusion.42 = f32[64,8,16,128]{3,0,2,1:T(8,128)S(1)} fusion(f32[64,8,16,128]{3,0,2,1:T(8,128)S(1)} %get-tuple-element.99, f32[64,8,16,128]{3,0,2,1:T(8,128)} %copy-done.3, f32[64,10,1,128]{3,0,2,1:T(8,128)S(1)} %collective-permute-done.23, f32[64,1,16,128]{3,0,2,1:T(8,128)S(1)} %collective-permute-done.21, f32[64,1,16,128]{3,0,2,1:T(8,128)S(1)} %collective-permute-done.20, ...), kind=kLoop, calls=%fused_computation.55 | loop fusion | flops 25165824 | bytes 14745600 | tf_op jit(solution)/shard_map/add | solution.py:41
  225.9 3.5 collective-permute-start.24
  230.7 6.0 %collective-permute-done.24 = f32[64,1,16,128]{3,0,2,1:T(8,128)S(1)} collective-permute-done((f32[64,1,16,128]{3,0,2,1:T(8,128)S(1)}, f32[64,1,16,128]{3,0,2,1:T(8,128)S(1)}, u32[]{:S(2)}, u32[]{:S(2)}) %collective-permute-start.24) | collective-permute-done | bytes 524320 | tf_op jit(solution)/shard_map/ppermute | solution.py:16
  236.7 4.1 collective-permute-done.25
  240.9 6.0 %collective-permute-start.26 = (f32[64,10,1,128]{3,0,2,1:T(8,128)S(1)}, f32[64,10,1,128]{3,0,2,1:T(8,128)S(1)}, u32[]{:S(2)}, u32[]{:S(2)}) collective-permute-start(f32[64,10,1,128]{3,0,2,1:T(8,128)S(1)} %get-tuple-element.107), channel_id=1, source_target_pairs={{0,1},{1,2},{2,3},{3,4},{4,5},{5,6},{6,7},{8,9},{9,10},{10,11},{11... | collective-permute-start | bytes 983048 | tf_op jit(solution)/shard_map/ppermute | solution.py:16
  250.9 4.4 collective-permute-done.27
  255.3 14.5 %fusion.97 = f32[64,8,16,128]{3,0,2,1:T(8,128)S(1)} fusion(f32[64,8,16,128]{3,0,2,1:T(8,128)} %copy-done, f32[64,8,16,128]{3,0,2,1:T(8,128)} %copy-done.2, f32[64,10,1,128]{3,0,2,1:T(8,128)S(1)} %collective-permute-done.27, f32[64,1,16,128]{3,0,2,1:T(8,128)S(1)} %collective-permute-done.25, f32[64,1,16,128]{3,0,2,1:T(8,128)S(1)} %collective-permute-done.24, ...), kind=kLoop, calls=%fused_computation.162 | loop fusion | flops 26214400 | bytes 14811136 | tf_op jit(solution)/shard_map/mul | solution.py:77
  271.8 3.4 fusion.98
  275.2 112.2 %psum.14 = f32[64,64]{0,1:T(8,128)S(1)} all-reduce(f32[64,64]{0,1:T(8,128)S(1)} %fusion.98), channel_id=1, replica_groups=mesh['gx'=32,'gy'=8] {'gx'}, use_global_device_ids=true, to_apply=%region_0.1 | all-reduce | flops 4096 | bytes 32768 | tf_op jit(solution)/shard_map/psum | solution.py:81
  387.4 44.3 %psum.15 = f32[64,64]{0,1:T(8,128)S(1)} all-reduce(f32[64,64]{0,1:T(8,128)S(1)} %psum.14), channel_id=1, replica_groups=mesh['gx'=32,'gy'=8] {'gy'}, use_global_device_ids=true, to_apply=%region_1.2 | all-reduce | flops 4096 | bytes 32768 | tf_op jit(solution)/shard_map/psum | solution.py:81
  431.8 5.8 %cholesky.19 = f32[64,64]{1,0:T(8,128)S(1)} custom-call(f32[64,64]{1,0:T(8,128)S(1)} %fusion.112), custom_call_target="Cholesky" | custom-call | tf_op jit(solution)/shard_map/jit(cholesky)/cholesky | solution.py:82
  439.7 6.6 %copy.29 = f32[64,8,16,128]{3,2,1,0:T(8,128)} copy(f32[64,8,16,128]{3,0,2,1:T(8,128)} %copy-done.1) | data formatting | bytes 8388608 | tf_op jit(solution)/shard_map/mul | solution.py:77
  447.0 90.6 %while.13 = (s32[]{:T(128)}, f32[64,64]{1,0:T(8,128)S(1)}, f32[64,64]{1,0:T(8,128)S(1)}, f32[64,64]{1,0:T(8,128)S(1)}, s32[]{:T(128)}, /*index=5*/s32[]{:T(128)}) while((s32[]{:T(128)}, f32[64,64]{1,0:T(8,128)S(1)}, f32[64,64]{1,0:T(8,128)S(1)}, f32[64,64]{1,0:T(8,128)S(1)}, s32[]{:T(128)}, /*index=5*/s32[]{:T(128)}) %tuple.57), condition=%wide.region_5.6_spmd, body=%wide.region_4.5_spmd.sunk | while | flops 49282 | bytes 36181 | solution.py:66
  537.5 4.6 copy.46
  542.8 6.0 %fusion.94 = f32[64,8,16,128]{3,0,2,1:T(8,128)S(1)} fusion(f32[8,16,128,64]{2,1,0,3:T(8,128)S(1)} %bitcast.44, f32[64,64]{1,0:T(8,128)S(1)} %get-tuple-element.81), kind=kOutput, calls=%fused_computation.156 | convolution fusion | flops 805306368 | bytes 8404992 | tf_op jit(solution)/shard_map/dot_general | solution.py:84
  548.8 4.4 copy.31
  (260 shorter events, 136.7 us)
Async XLA Ops:
  1.3 5.7 %collective-permute-start = (f32[1,16,128]{2,1,0:T(8,128)S(1)}, f32[1,16,128]{2,1,0:T(8,128)S(1)}, u32[]{:S(2)}, u32[]{:S(2)}) collective-permute-start(f32[1,16,128]{2,1,0:T(8,128)S(1)} %get-tuple-element.134), channel_id=1, source_target_pairs={{0,8},{8,16},{16,24},{24,32},{32,40},{40,48},{48,56},{56,64},{64,7... | collective-permute-start | bytes 24584 | tf_op jit(solution)/shard_map/ppermute | solution.py:16
  5.7 4.6 collective-permute-start.1
  10.3 6.9 %collective-permute-start.2 = (f32[10,1,128]{2,1,0:T(1,128)S(1)}, f32[10,1,128]{2,1,0:T(1,128)S(1)}, u32[]{:S(2)}, u32[]{:S(2)}) collective-permute-start(f32[10,1,128]{2,1,0:T(1,128)S(1)} %get-tuple-element.132), channel_id=1, source_target_pairs={{0,1},{1,2},{2,3},{3,4},{4,5},{5,6},{6,7},{8,9},{9,10},{10,11},{11... | collective-permute-start | bytes 15368 | tf_op jit(solution)/shard_map/ppermute | solution.py:16
  15.3 4.9 collective-permute-start.3
  24.8 31.6 %copy-start.5 = (bf16[64,8,16,128]{3,2,1,0:T(8,128)(2,1)S(1)}, bf16[64,8,16,128]{3,2,1,0:T(8,128)(2,1)}, u32[]{:S(2)}) copy-start(bf16[64,8,16,128]{3,2,1,0:T(8,128)(2,1)} %param.7) | copy-start | bytes 6291460
  24.8 31.6 %copy-start.6 = (f32[8,16,128]{2,1,0:T(8,128)S(1)}, f32[8,16,128]{2,1,0:T(8,128)}, u32[]{:S(2)}) copy-start(f32[8,16,128]{2,1,0:T(8,128)} %param.10) | copy-start | bytes 196612
  24.9 14.0 %collective-permute-start.4 = (f32[64,1,16,128]{3,0,2,1:T(8,128)S(1)}, f32[64,1,16,128]{3,0,2,1:T(8,128)S(1)}, u32[]{:S(2)}, u32[]{:S(2)}) collective-permute-start(f32[64,1,16,128]{3,0,2,1:T(8,128)S(1)} %get-tuple-element.129), channel_id=1, source_target_pairs={{0,8},{8,16},{16,24},{24,32},{32,40},{40,48},{48,56},{56,64},{64,7... | collective-permute-start | bytes 1572872 | tf_op jit(solution)/shard_map/ppermute | solution.py:16
  28.6 15.4 %collective-permute-start.5 = (f32[64,1,16,128]{3,0,2,1:T(8,128)S(1)}, f32[64,1,16,128]{3,0,2,1:T(8,128)S(1)}, u32[]{:S(2)}, u32[]{:S(2)}) collective-permute-start(f32[64,1,16,128]{3,0,2,1:T(8,128)S(1)} %get-tuple-element.130), channel_id=1, source_target_pairs={{8,0},{16,8},{24,16},{32,24},{40,32},{48,40},{56,48},{64,56},{72,6... | collective-permute-start | bytes 1572872 | tf_op jit(solution)/shard_map/ppermute | solution.py:17
  44.1 7.9 %collective-permute-start.6 = (f32[64,10,1,128]{3,0,2,1:T(8,128)S(1)}, f32[64,10,1,128]{3,0,2,1:T(8,128)S(1)}, u32[]{:S(2)}, u32[]{:S(2)}) collective-permute-start(f32[64,10,1,128]{3,0,2,1:T(8,128)S(1)} %get-tuple-element.117), channel_id=1, source_target_pairs={{0,1},{1,2},{2,3},{3,4},{4,5},{5,6},{6,7},{8,9},{9,10},{10,11},{11... | collective-permute-start | bytes 983048 | tf_op jit(solution)/shard_map/ppermute | solution.py:16
  48.0 8.4 %collective-permute-start.7 = (f32[64,10,1,128]{3,0,2,1:T(8,128)S(1)}, f32[64,10,1,128]{3,0,2,1:T(8,128)S(1)}, u32[]{:S(2)}, u32[]{:S(2)}) collective-permute-start(f32[64,10,1,128]{3,0,2,1:T(8,128)S(1)} %get-tuple-element.118), channel_id=1, source_target_pairs={{1,0},{2,1},{3,2},{4,3},{5,4},{6,5},{7,6},{9,8},{10,9},{11,10},{12... | collective-permute-start | bytes 983048 | tf_op jit(solution)/shard_map/ppermute | solution.py:17
  64.3 12.2 %collective-permute-start.8 = (f32[64,1,16,128]{3,0,2,1:T(8,128)S(1)}, f32[64,1,16,128]{3,0,2,1:T(8,128)S(1)}, u32[]{:S(2)}, u32[]{:S(2)}) collective-permute-start(f32[64,1,16,128]{3,0,2,1:T(8,128)S(1)} %get-tuple-element.127), channel_id=1, source_target_pairs={{0,8},{8,16},{16,24},{24,32},{32,40},{40,48},{48,56},{56,64},{64,7... | collective-permute-start | bytes 1572872 | tf_op jit(solution)/shard_map/ppermute | solution.py:16
  69.2 11.7 %collective-permute-start.9 = (f32[64,1,16,128]{3,0,2,1:T(8,128)S(1)}, f32[64,1,16,128]{3,0,2,1:T(8,128)S(1)}, u32[]{:S(2)}, u32[]{:S(2)}) collective-permute-start(f32[64,1,16,128]{3,0,2,1:T(8,128)S(1)} %get-tuple-element.128), channel_id=1, source_target_pairs={{8,0},{16,8},{24,16},{32,24},{40,32},{48,40},{56,48},{64,56},{72,6... | collective-permute-start | bytes 1572872 | tf_op jit(solution)/shard_map/ppermute | solution.py:17
  81.0 10.2 %collective-permute-start.10 = (f32[64,10,1,128]{3,0,2,1:T(8,128)S(1)}, f32[64,10,1,128]{3,0,2,1:T(8,128)S(1)}, u32[]{:S(2)}, u32[]{:S(2)}) collective-permute-start(f32[64,10,1,128]{3,0,2,1:T(8,128)S(1)} %get-tuple-element.115), channel_id=1, source_target_pairs={{0,1},{1,2},{2,3},{3,4},{4,5},{5,6},{6,7},{8,9},{9,10},{10,11},{11... | collective-permute-start | bytes 983048 | tf_op jit(solution)/shard_map/ppermute | solution.py:16
  87.2 8.4 %collective-permute-start.11 = (f32[64,10,1,128]{3,0,2,1:T(8,128)S(1)}, f32[64,10,1,128]{3,0,2,1:T(8,128)S(1)}, u32[]{:S(2)}, u32[]{:S(2)}) collective-permute-start(f32[64,10,1,128]{3,0,2,1:T(8,128)S(1)} %get-tuple-element.116), channel_id=1, source_target_pairs={{1,0},{2,1},{3,2},{4,3},{5,4},{6,5},{7,6},{9,8},{10,9},{11,10},{12... | collective-permute-start | bytes 983048 | tf_op jit(solution)/shard_map/ppermute | solution.py:17
  103.4 30.7 %copy-start.7 = (f32[8,16,128]{2,1,0:T(8,128)S(1)}, f32[8,16,128]{2,1,0:T(8,128)}, u32[]{:S(2)}) copy-start(f32[8,16,128]{2,1,0:T(8,128)} %param.11) | copy-start | bytes 196612
  103.5 11.3 %collective-permute-start.12 = (f32[64,1,16,128]{3,0,2,1:T(8,128)S(1)}, f32[64,1,16,128]{3,0,2,1:T(8,128)S(1)}, u32[]{:S(2)}, u32[]{:S(2)}) collective-permute-start(f32[64,1,16,128]{3,0,2,1:T(8,128)S(1)} %get-tuple-element.125), channel_id=1, source_target_pairs={{0,8},{8,16},{16,24},{24,32},{32,40},{40,48},{48,56},{56,64},{64,7... | collective-permute-start | bytes 1572872 | tf_op jit(solution)/shard_map/ppermute | solution.py:16
  107.5 11.4 %collective-permute-start.13 = (f32[64,1,16,128]{3,0,2,1:T(8,128)S(1)}, f32[64,1,16,128]{3,0,2,1:T(8,128)S(1)}, u32[]{:S(2)}, u32[]{:S(2)}) collective-permute-start(f32[64,1,16,128]{3,0,2,1:T(8,128)S(1)} %get-tuple-element.126), channel_id=1, source_target_pairs={{8,0},{16,8},{24,16},{32,24},{40,32},{48,40},{56,48},{64,56},{72,6... | collective-permute-start | bytes 1572872 | tf_op jit(solution)/shard_map/ppermute | solution.py:17
  119.0 10.7 %collective-permute-start.14 = (f32[64,10,1,128]{3,0,2,1:T(8,128)S(1)}, f32[64,10,1,128]{3,0,2,1:T(8,128)S(1)}, u32[]{:S(2)}, u32[]{:S(2)}) collective-permute-start(f32[64,10,1,128]{3,0,2,1:T(8,128)S(1)} %get-tuple-element.113), channel_id=1, source_target_pairs={{0,1},{1,2},{2,3},{3,4},{4,5},{5,6},{6,7},{8,9},{9,10},{10,11},{11... | collective-permute-start | bytes 983048 | tf_op jit(solution)/shard_map/ppermute | solution.py:16
  125.7 8.4 %collective-permute-start.15 = (f32[64,10,1,128]{3,0,2,1:T(8,128)S(1)}, f32[64,10,1,128]{3,0,2,1:T(8,128)S(1)}, u32[]{:S(2)}, u32[]{:S(2)}) collective-permute-start(f32[64,10,1,128]{3,0,2,1:T(8,128)S(1)} %get-tuple-element.114), channel_id=1, source_target_pairs={{1,0},{2,1},{3,2},{4,3},{5,4},{6,5},{7,6},{9,8},{10,9},{11,10},{12... | collective-permute-start | bytes 983048 | tf_op jit(solution)/shard_map/ppermute | solution.py:17
  142.0 29.3 %copy-start.4 = (f32[64,8,16,128]{3,0,2,1:T(8,128)}, f32[64,8,16,128]{3,0,2,1:T(8,128)S(1)}, u32[]{:S(2)}) copy-start(f32[64,8,16,128]{3,0,2,1:T(8,128)S(1)} %get-tuple-element.98) | copy-start | bytes 12582916
  142.1 70.6 %copy-start = (f32[64,8,16,128]{3,0,2,1:T(8,128)}, f32[64,8,16,128]{3,0,2,1:T(8,128)S(1)}, u32[]{:S(2)}) copy-start(f32[64,8,16,128]{3,0,2,1:T(8,128)S(1)} %get-tuple-element.99) | copy-start | bytes 12582916
  142.1 9.4 %collective-permute-start.16 = (f32[64,1,16,128]{3,0,2,1:T(8,128)S(1)}, f32[64,1,16,128]{3,0,2,1:T(8,128)S(1)}, u32[]{:S(2)}, u32[]{:S(2)}) collective-permute-start(f32[64,1,16,128]{3,0,2,1:T(8,128)S(1)} %get-tuple-element.123), channel_id=1, source_target_pairs={{0,8},{8,16},{16,24},{24,32},{32,40},{40,48},{48,56},{56,64},{64,7... | collective-permute-start | bytes 1572872 | tf_op jit(solution)/shard_map/ppermute | solution.py:16
  144.2 11.4 %collective-permute-start.17 = (f32[64,1,16,128]{3,0,2,1:T(8,128)S(1)}, f32[64,1,16,128]{3,0,2,1:T(8,128)S(1)}, u32[]{:S(2)}, u32[]{:S(2)}) collective-permute-start(f32[64,1,16,128]{3,0,2,1:T(8,128)S(1)} %get-tuple-element.124), channel_id=1, source_target_pairs={{8,0},{16,8},{24,16},{32,24},{40,32},{48,40},{56,48},{64,56},{72,6... | collective-permute-start | bytes 1572872 | tf_op jit(solution)/shard_map/ppermute | solution.py:17
  155.7 11.3 %collective-permute-start.18 = (f32[64,10,1,128]{3,0,2,1:T(8,128)S(1)}, f32[64,10,1,128]{3,0,2,1:T(8,128)S(1)}, u32[]{:S(2)}, u32[]{:S(2)}) collective-permute-start(f32[64,10,1,128]{3,0,2,1:T(8,128)S(1)} %get-tuple-element.111), channel_id=1, source_target_pairs={{0,1},{1,2},{2,3},{3,4},{4,5},{5,6},{6,7},{8,9},{9,10},{10,11},{11... | collective-permute-start | bytes 983048 | tf_op jit(solution)/shard_map/ppermute | solution.py:16
  163.0 8.4 %collective-permute-start.19 = (f32[64,10,1,128]{3,0,2,1:T(8,128)S(1)}, f32[64,10,1,128]{3,0,2,1:T(8,128)S(1)}, u32[]{:S(2)}, u32[]{:S(2)}) collective-permute-start(f32[64,10,1,128]{3,0,2,1:T(8,128)S(1)} %get-tuple-element.112), channel_id=1, source_target_pairs={{1,0},{2,1},{3,2},{4,3},{5,4},{6,5},{7,6},{9,8},{10,9},{11,10},{12... | collective-permute-start | bytes 983048 | tf_op jit(solution)/shard_map/ppermute | solution.py:17
  184.5 23.7 %copy-start.3 = (f32[64,8,16,128]{3,0,2,1:T(8,128)}, f32[64,8,16,128]{3,0,2,1:T(8,128)S(1)}, u32[]{:S(2)}) copy-start(f32[64,8,16,128]{3,0,2,1:T(8,128)S(1)} %fusion.34) | copy-start | bytes 12582916
  184.6 8.5 %collective-permute-start.20 = (f32[64,1,16,128]{3,0,2,1:T(8,128)S(1)}, f32[64,1,16,128]{3,0,2,1:T(8,128)S(1)}, u32[]{:S(2)}, u32[]{:S(2)}) collective-permute-start(f32[64,1,16,128]{3,0,2,1:T(8,128)S(1)} %get-tuple-element.121), channel_id=1, source_target_pairs={{0,8},{8,16},{16,24},{24,32},{32,40},{40,48},{48,56},{56,64},{64,7... | collective-permute-start | bytes 1572872 | tf_op jit(solution)/shard_map/ppermute | solution.py:16
  186.0 11.3 %collective-permute-start.21 = (f32[64,1,16,128]{3,0,2,1:T(8,128)S(1)}, f32[64,1,16,128]{3,0,2,1:T(8,128)S(1)}, u32[]{:S(2)}, u32[]{:S(2)}) collective-permute-start(f32[64,1,16,128]{3,0,2,1:T(8,128)S(1)} %get-tuple-element.122), channel_id=1, source_target_pairs={{8,0},{16,8},{24,16},{32,24},{40,32},{48,40},{56,48},{64,56},{72,6... | collective-permute-start | bytes 1572872 | tf_op jit(solution)/shard_map/ppermute | solution.py:17
  197.4 10.9 %collective-permute-start.22 = (f32[64,10,1,128]{3,0,2,1:T(8,128)S(1)}, f32[64,10,1,128]{3,0,2,1:T(8,128)S(1)}, u32[]{:S(2)}, u32[]{:S(2)}) collective-permute-start(f32[64,10,1,128]{3,0,2,1:T(8,128)S(1)} %get-tuple-element.109), channel_id=1, source_target_pairs={{0,1},{1,2},{2,3},{3,4},{4,5},{5,6},{6,7},{8,9},{9,10},{10,11},{11... | collective-permute-start | bytes 983048 | tf_op jit(solution)/shard_map/ppermute | solution.py:16
  204.3 8.4 %collective-permute-start.23 = (f32[64,10,1,128]{3,0,2,1:T(8,128)S(1)}, f32[64,10,1,128]{3,0,2,1:T(8,128)S(1)}, u32[]{:S(2)}, u32[]{:S(2)}) collective-permute-start(f32[64,10,1,128]{3,0,2,1:T(8,128)S(1)} %get-tuple-element.110), channel_id=1, source_target_pairs={{1,0},{2,1},{3,2},{4,3},{5,4},{6,5},{7,6},{9,8},{10,9},{11,10},{12... | collective-permute-start | bytes 983048 | tf_op jit(solution)/shard_map/ppermute | solution.py:17
  225.8 15.0 %copy-start.2 = (f32[64,8,16,128]{3,0,2,1:T(8,128)}, f32[64,8,16,128]{3,0,2,1:T(8,128)S(1)}, u32[]{:S(2)}) copy-start(f32[64,8,16,128]{3,0,2,1:T(8,128)S(1)} %fusion.42) | copy-start | bytes 12582916
  225.9 10.8 %collective-permute-start.24 = (f32[64,1,16,128]{3,0,2,1:T(8,128)S(1)}, f32[64,1,16,128]{3,0,2,1:T(8,128)S(1)}, u32[]{:S(2)}, u32[]{:S(2)}) collective-permute-start(f32[64,1,16,128]{3,0,2,1:T(8,128)S(1)} %get-tuple-element.119), channel_id=1, source_target_pairs={{0,8},{8,16},{16,24},{24,32},{32,40},{40,48},{48,56},{56,64},{64,7... | collective-permute-start | bytes 1572872 | tf_op jit(solution)/shard_map/ppermute | solution.py:16
  229.4 11.4 %collective-permute-start.25 = (f32[64,1,16,128]{3,0,2,1:T(8,128)S(1)}, f32[64,1,16,128]{3,0,2,1:T(8,128)S(1)}, u32[]{:S(2)}, u32[]{:S(2)}) collective-permute-start(f32[64,1,16,128]{3,0,2,1:T(8,128)S(1)} %get-tuple-element.120), channel_id=1, source_target_pairs={{8,0},{16,8},{24,16},{32,24},{40,32},{48,40},{56,48},{64,56},{72,6... | collective-permute-start | bytes 1572872 | tf_op jit(solution)/shard_map/ppermute | solution.py:17
  240.9 10.0 %collective-permute-start.26 = (f32[64,10,1,128]{3,0,2,1:T(8,128)S(1)}, f32[64,10,1,128]{3,0,2,1:T(8,128)S(1)}, u32[]{:S(2)}, u32[]{:S(2)}) collective-permute-start(f32[64,10,1,128]{3,0,2,1:T(8,128)S(1)} %get-tuple-element.107), channel_id=1, source_target_pairs={{0,1},{1,2},{2,3},{3,4},{4,5},{5,6},{6,7},{8,9},{9,10},{10,11},{11... | collective-permute-start | bytes 983048 | tf_op jit(solution)/shard_map/ppermute | solution.py:16
  246.9 8.4 %collective-permute-start.27 = (f32[64,10,1,128]{3,0,2,1:T(8,128)S(1)}, f32[64,10,1,128]{3,0,2,1:T(8,128)S(1)}, u32[]{:S(2)}, u32[]{:S(2)}) collective-permute-start(f32[64,10,1,128]{3,0,2,1:T(8,128)S(1)} %get-tuple-element.108), channel_id=1, source_target_pairs={{1,0},{2,1},{3,2},{4,3},{5,4},{6,5},{7,6},{9,8},{10,9},{11,10},{12... | collective-permute-start | bytes 983048 | tf_op jit(solution)/shard_map/ppermute | solution.py:17
  269.8 2.0 copy-start.1
